TPU v7x, 32 devices: a whole 2x2x4 slice. The times are simulated.
32 devices in a mesh: lon: 4 (over x, core), lat: 8 (over z, y).
Axes of the slice: x: 2, y: 2, z: 4, core: 2. Of those that a mesh axis runs over, the one named last changes fastest.
Arguments:
- model_state: float32 [4, 8, 256, 5760], P(None, None, 'lat', 'lon')
- courant: float32 [256], P('lat'), may hold values from 0.02 to 0.08
- cutoff: int32 [256], replicated, may hold values from 1 to 2880, as said below
Outputs:
- new_state: float32 [4, 8, 256, 5760], P(None, None, 'lat', 'lon')
Inputs may be any that keep to these rules, and one draw needn't show every extreme that they name: `cutoff`: rows 64 to 191 hold 5760/2 (no damping); every other row holds less.
All inputs are finite; a program needn't handle non-finite values.
Results may differ from a plain program's by a relative error of at most 0.000073.
Values sent between devices are 32-bit elements; how exact they have to be, the bound alone decides.
A program may use at most 64 MiB of HBM per device.

v0:
```python
import functools

import jax
import jax.numpy as jnp
import numpy as np
from jax import lax
from jax.experimental import pallas as pl
from jax.experimental.pallas import tpu as pltpu
from jax.sharding import PartitionSpec as P

meridional_courant = 0.05
pressure_gain = 4.0
MESH = pl.DeviceIdType.MESH


def with_halo(array, sides, width):
    for axis, dim in sides:
        size, length = (lax.axis_size(axis), array.shape[dim])
        up = [(i, (i + 1) % size) for i in range(size)]
        down = [(j, i) for i, j in up]
        last = lax.slice_in_dim(array, length - width, length, axis=dim)
        first = lax.slice_in_dim(array, 0, width, axis=dim)
        before = lax.ppermute(last, axis, up)
        after = lax.ppermute(first, axis, down)
        array = jnp.concatenate([before, array, after], axis=dim)
    return array


def quarter_basis(quarter):
    half = quarter // 2
    lanes = -(-(half + 1) // 128) * 128
    phase = np.outer(np.arange(quarter), np.arange(half + 1)) % quarter
    angle = 2.0 * np.pi / quarter * phase
    table = np.zeros((quarter, 2 * lanes), np.float32)
    table[:, : half + 1] = np.cos(angle)
    table[:, lanes : lanes + half + 1] = np.sin(angle)
    return table


def quarter_twists(quarter):
    angle = 2.0 * np.pi / (4 * quarter) * np.outer([1.0, 2.0], np.arange(quarter))
    return np.cos(angle).astype(np.float32), np.sin(angle).astype(np.float32)


def damping_tables(row_cutoff, quarter):
    half = quarter // 2
    length = 4 * quarter
    lanes = -(-(half + 1) // 128) * 128
    index = jnp.arange(lanes, dtype=jnp.int32)
    inside = index <= half
    weight = jnp.where(inside, jnp.where((index == 0) | (index == half), 1.0, 2.0), 0.0) / quarter
    cut = row_cutoff.astype(jnp.float32)[:, None]

    def damping(wave_number):
        wave_number = jnp.abs(wave_number)
        folded = jnp.minimum(wave_number, length - wave_number)
        ratio = cut / jnp.maximum(folded, 1).astype(jnp.float32)[None, :]
        return jnp.minimum(1.0, ratio * ratio)

    def pair(shift, scale):
        above = damping(4 * index + shift)
        below = damping(4 * index - shift)
        gain = weight[None, :] * (0.5 * scale)
        return gain * (above + below), gain * (above - below)

    return pair(0, 0.25)[0], pair(2, 0.25), pair(1, 0.5)


def mix(real_cos, real_sin, imag_cos, imag_sin, same, cross):
    return (
        same * real_cos + cross * imag_sin,
        same * real_sin - cross * imag_cos,
        same * imag_cos - cross * real_sin,
        same * imag_sin + cross * real_cos,
    )


def damp_quarters(quarters, row_cutoff):
    _, planes, rows, quarter = quarters.shape
    basis = jnp.asarray(quarter_basis(quarter))
    cos_twist, sin_twist = quarter_twists(quarter)
    q0, q1, q2, q3 = quarters
    even, odd_a, odd_b = (q0 + q2) + (q1 + q3), q0 - q2, q1 - q3
    skew = (q0 + q2) - (q1 + q3)
    pairs = planes // 2
    skew_a, skew_b = skew[:pairs], skew[pairs:]
    one_real = odd_a * cos_twist[0] - odd_b * sin_twist[0]
    one_imag = -odd_a * sin_twist[0] - odd_b * cos_twist[0]
    two_real = skew_a * cos_twist[1] + skew_b * sin_twist[1]
    two_imag = skew_b * cos_twist[1] - skew_a * sin_twist[1]
    stack = jnp.concatenate([even, two_real, two_imag, one_real, one_imag], axis=0)
    waves = jnp.einsum("prm,mk->prk", stack, basis, precision=lax.Precision.HIGH)
    lanes = basis.shape[1] // 2
    cos_part, sin_part = waves[..., :lanes], waves[..., lanes:]
    same0, (same2, cross2), (same1, cross1) = damping_tables(row_cutoff, quarter)
    p, h = planes, pairs
    two = slice(p, p + h), slice(p + h, 2 * p)
    one = slice(2 * p, 3 * p), slice(3 * p, 4 * p)
    even_c, even_s = same0 * cos_part[:p], same0 * sin_part[:p]
    rc2, rs2, ic2, is2 = mix(
        cos_part[two[0]], sin_part[two[0]], cos_part[two[1]], sin_part[two[1]], same2, cross2
    )
    rc1, rs1, ic1, is1 = mix(
        cos_part[one[0]], sin_part[one[0]], cos_part[one[1]], sin_part[one[1]], same1, cross1
    )
    damped = jnp.concatenate(
        [
            jnp.concatenate([even_c, rc2, ic2, rc1, ic1], axis=0),
            jnp.concatenate([even_s, rs2, is2, rs1, is1], axis=0),
        ],
        axis=-1,
    )
    back = jnp.einsum("prk,mk->prm", damped, basis, precision=lax.Precision.HIGH)
    even, two_real, two_imag = back[:p], back[two[0]], back[two[1]]
    one_real, one_imag = back[one[0]], back[one[1]]
    odd_a = one_real * cos_twist[0] - one_imag * sin_twist[0]
    odd_b = -one_real * sin_twist[0] - one_imag * cos_twist[0]
    skew = jnp.concatenate(
        [
            two_real * cos_twist[1] - two_imag * sin_twist[1],
            two_imag * cos_twist[1] + two_real * sin_twist[1],
        ],
        axis=0,
    )
    plus, minus = even + skew, even - skew
    return jnp.stack([plus + odd_a, minus + odd_b, plus - odd_a, minus - odd_b])


def trim_rims(extended, row_dim):
    band_index = lax.axis_index("lat")
    band_count = lax.axis_size("lat")
    rows_ext = extended.shape[row_dim]
    positions = jnp.arange(rows_ext, dtype=jnp.int32)
    keep_rows = jnp.logical_not(
        (positions == 0) & (band_index == 0)
        | (positions == rows_ext - 1) & (band_index == band_count - 1)
    )
    mask_shape = [1] * extended.ndim
    mask_shape[row_dim] = rows_ext
    return extended * keep_rows.astype(extended.dtype).reshape(mask_shape)


def along_lon(field_ext):
    return (field_ext[..., 1:-1, 2:] - field_ext[..., 1:-1, :-2]) * 0.5


def along_lat(field_ext):
    return (field_ext[..., 2:, 1:-1] - field_ext[..., :-2, 1:-1]) * 0.5


def filter_block(work_block, block_cutoff):
    lon_parts = lax.axis_size("lon")
    components, levels, rows_here, width_here = work_block.shape
    planes = components * levels // lon_parts
    group = lon_parts // 4
    lines = work_block.reshape(lon_parts, planes, rows_here, width_here)
    circles = lax.all_to_all(lines, "lon", split_axis=0, concat_axis=0, tiled=True)
    quarters = circles.reshape(4, group, planes, rows_here, width_here)
    quarters = jnp.moveaxis(quarters, 1, 3).reshape(4, planes, rows_here, group * width_here)
    smoothed = damp_quarters(quarters, block_cutoff)
    smoothed = smoothed.reshape(4, planes, rows_here, group, width_here)
    smoothed = jnp.moveaxis(smoothed, 3, 1).reshape(lines.shape)
    returned = lax.all_to_all(smoothed, "lon", split_axis=0, concat_axis=0, tiled=True)
    return returned.reshape(work_block.shape)


def worker_group(band, bands):
    quarter = bands // 4
    low = band < bands // 2
    polar = jnp.logical_or(band < quarter, band >= bands - quarter)
    inner = jnp.where(low, band - quarter, band + quarter)
    source = jnp.where(polar, band, inner)
    helper = jnp.where(source < bands // 2, source + quarter, source - quarter)
    return polar, source, helper


def split_store(ref, values):
    rows, width = values.shape
    high = values.astype(jnp.bfloat16)
    low = (values - high.astype(jnp.float32)).astype(jnp.bfloat16)
    ref[:rows, :width] = high
    ref[rows:, :width] = low


def product(parts, high_ref, low_ref, out_ref, back):
    rows = out_ref.shape[0]
    dims = (((1,), (1 if back else 0,)), ((), ()))
    for start in range(0, out_ref.shape[1], 256):
        cols = slice(start, start + 256)
        piece = (cols, slice(None)) if back else (slice(None), cols)
        both = lax.dot_general(parts[...], high_ref[piece], dims, preferred_element_type=jnp.float32)
        cross = lax.dot_general(
            parts[:rows, :], low_ref[piece], dims, preferred_element_type=jnp.float32
        )
        out_ref[:, cols] = (both[:rows] + both[rows:]) + cross


def circle_kernel(
    bands, parts, chunks, state, gains, twists, tables, out, circles, results, high, low, operand, waves,
    send_sem, recv_sem, back_send_sem, back_recv_sem, local_sem,
):
    part = lax.axis_index("lon")
    band = lax.axis_index("lat")
    polar, source, helper = worker_group(band, bands)
    _, _, per, rows, quarter = circles.shape
    width = high.shape[1]
    lanes = width // 2
    workers = 2 * parts
    row_chunks = state.shape[1] // rows
    planes_per = state.shape[0] // workers
    me = jnp.where(polar, part, part + parts)

    def block(ref, worker, chunk):
        plane = worker * planes_per + (chunk // row_chunks) * per
        row = pl.multiple_of((chunk % row_chunks) * rows, rows)
        return ref.at[pl.ds(plane, per), pl.ds(row, rows), :]

    barrier = pltpu.get_barrier_semaphore()
    for step in range(1, parts):
        @pl.when(polar)
        def _():
            pl.semaphore_signal(
                barrier, inc=1, device_id=(lax.rem(part + step, parts), band), device_id_type=MESH
            )
    for step in range(parts):
        pl.semaphore_signal(
            barrier,
            inc=1,
            device_id=(lax.rem(part + step, parts), jnp.where(polar, helper, source)),
            device_id_type=MESH,
        )

    loads = [
        pltpu.make_async_copy(tables.at[i], ref, local_sem.at[i])
        for i, ref in enumerate((high, low))
    ]
    for load in loads:
        load.start()
    through = pltpu.make_async_copy(state, out, local_sem.at[2])

    @pl.when(jnp.logical_not(polar))
    def _():
        through.start()
        pl.semaphore_wait(barrier, parts)

    @pl.when(polar)
    def _():
        pl.semaphore_wait(barrier, 2 * parts - 1)

        @pl.loop(0, chunks)
        def _(chunk):
            for step in range(parts):
                there = lax.rem(part + step, parts)
                pltpu.make_async_remote_copy(
                    src_ref=block(state, there + parts, chunk),
                    dst_ref=circles.at[chunk, part],
                    send_sem=send_sem.at[chunk, there + parts],
                    recv_sem=recv_sem.at[chunk, part],
                    device_id=(there, helper),
                    device_id_type=MESH,
                ).start()
                if step == 0:
                    pltpu.make_async_copy(
                        block(state, me, chunk), circles.at[chunk, part], recv_sem.at[chunk, part]
                    ).start()
                else:
                    pltpu.make_async_remote_copy(
                        src_ref=block(state, there, chunk),
                        dst_ref=circles.at[chunk, part],
                        send_sem=send_sem.at[chunk, there],
                        recv_sem=recv_sem.at[chunk, part],
                        device_id=(there, band),
                        device_id_type=MESH,
                    ).start()

    operand[...] = jnp.zeros_like(operand)
    for load in loads:
        load.wait()
    cos1, sin1, cos2, sin2 = (twists[i : i + 1, :] for i in range(4))
    half, whole = rows, per * rows

    @pl.loop(0, chunks)
    def _(chunk):
        for i in range(parts):
            slot = circles.at[chunk, i]
            pltpu.make_async_copy(slot, slot, recv_sem.at[chunk, i]).wait()
        q0, q1, q2, q3 = (circles[chunk, i].reshape(whole, quarter) for i in range(4))
        sum_a, sum_b, odd_a, odd_b = q0 + q2, q1 + q3, q0 - q2, q1 - q3
        skew = sum_a - sum_b
        skew_a, skew_b = skew[:half], skew[half:]
        stack = jnp.concatenate(
            [
                sum_a + sum_b,
                skew_a * cos2 + skew_b * sin2,
                skew_b * cos2 - skew_a * sin2,
                odd_a * cos1 - odd_b * sin1,
                -odd_a * sin1 - odd_b * cos1,
            ],
            axis=0,
        )
        split_store(operand, stack)
        product(operand, high, low, waves, False)
        row = pl.multiple_of((chunk % row_chunks) * rows, rows)
        g = [gains[i, pl.ds(row, rows), :] for i in range(5)]
        same0, same2, cross2, same1, cross1 = (
            g[0], g[1], g[2], jnp.concatenate([g[3]] * per), jnp.concatenate([g[4]] * per)
        )
        same0 = jnp.concatenate([same0] * per)
        cos_part, sin_part = waves[:, :lanes], waves[:, lanes:]
        two_a, two_b = slice(whole, whole + half), slice(whole + half, 2 * whole)
        one_a, one_b = slice(2 * whole, 3 * whole), slice(3 * whole, 4 * whole)
        rc2, rs2, ic2, is2 = mix(
            cos_part[two_a], sin_part[two_a], cos_part[two_b], sin_part[two_b], same2, cross2
        )
        rc1, rs1, ic1, is1 = mix(
            cos_part[one_a], sin_part[one_a], cos_part[one_b], sin_part[one_b], same1, cross1
        )
        damped = jnp.concatenate(
            [
                jnp.concatenate([same0 * cos_part[:whole], rc2, ic2, rc1, ic1], axis=0),
                jnp.concatenate([same0 * sin_part[:whole], rs2, is2, rs1, is1], axis=0),
            ],
            axis=1,
        )
        split_store(operand, damped)
        product(operand, high, low, waves, True)
        back = waves[:, :quarter]
        even, two_real, two_imag = back[:whole], back[two_a], back[two_b]
        one_real, one_imag = back[one_a], back[one_b]
        odd_a = one_real * cos1 - one_imag * sin1
        odd_b = -one_real * sin1 - one_imag * cos1
        skew = jnp.concatenate(
            [two_real * cos2 - two_imag * sin2, two_imag * cos2 + two_real * sin2], axis=0
        )
        plus, minus = even + skew, even - skew
        shape = (per, rows, quarter)
        results[chunk, 0] = (plus + odd_a).reshape(shape)
        results[chunk, 1] = (minus + odd_b).reshape(shape)
        results[chunk, 2] = (plus - odd_a).reshape(shape)
        results[chunk, 3] = (minus - odd_b).reshape(shape)
        if quarter < width:
            operand[:, quarter:] = jnp.zeros_like(operand[:, quarter:])
        for step in range(1, parts):
            there = lax.rem(part + step, parts)
            pltpu.make_async_remote_copy(
                src_ref=results.at[chunk, there],
                dst_ref=block(out, me, chunk),
                send_sem=back_send_sem.at[chunk, there],
                recv_sem=back_recv_sem.at[chunk, me],
                device_id=(there, source),
                device_id_type=MESH,
            ).start()

        @pl.when(polar)
        def _():
            pltpu.make_async_copy(
                results.at[chunk, part], block(out, me, chunk), back_recv_sem.at[chunk, me]
            ).start()

        @pl.when(jnp.logical_not(polar))
        def _():
            pltpu.make_async_remote_copy(
                src_ref=results.at[chunk, part],
                dst_ref=block(out, me, chunk),
                send_sem=back_send_sem.at[chunk, part],
                recv_sem=back_recv_sem.at[chunk, me],
                device_id=(part, source),
                device_id_type=MESH,
            ).start()

    def drain(ref, semaphore):
        pltpu.make_async_copy(ref, ref, semaphore).wait()

    @pl.loop(0, chunks)
    def _(chunk):
        for step in range(1, parts):
            there = lax.rem(part + step, parts)
            drain(results.at[chunk, there], back_send_sem.at[chunk, there])

        @pl.when(jnp.logical_not(polar))
        def _():
            drain(results.at[chunk, part], back_send_sem.at[chunk, part])

        @pl.when(polar)
        def _():
            for step in range(parts):
                there = lax.rem(part + step, parts)
                drain(block(state, there + parts, chunk), send_sem.at[chunk, there + parts])
                drain(block(out, there + parts, chunk), back_recv_sem.at[chunk, there + parts])
                drain(block(out, there, chunk), back_recv_sem.at[chunk, there])
                if step > 0:
                    drain(block(state, there, chunk), send_sem.at[chunk, there])

    @pl.when(jnp.logical_not(polar))
    def _():
        through.wait()


def shared_filter(work_block, cutoff):
    parts, bands = lax.axis_size("lon"), lax.axis_size("lat")
    components, levels, rows_here, quarter = work_block.shape
    state = work_block.reshape(components * levels, rows_here, quarter)
    per, rows = 2, 16
    chunks = (components * levels // (2 * parts) // per) * (rows_here // rows)
    basis = quarter_basis(quarter)
    width = basis.shape[1]
    square = np.zeros((width, width), np.float32)
    square[:quarter] = basis
    high = square.astype(jnp.bfloat16)
    low = (square - high.astype(np.float32)).astype(jnp.bfloat16)
    tables = jnp.asarray(np.stack([high, low]))
    cos_twist, sin_twist = quarter_twists(quarter)
    twists = jnp.asarray(np.stack([cos_twist[0], sin_twist[0], cos_twist[1], sin_twist[1]]))
    _, source, _ = worker_group(lax.axis_index("lat"), bands)
    row_cutoff = lax.dynamic_slice_in_dim(cutoff, source * rows_here, rows_here)
    same0, two, one = damping_tables(row_cutoff, quarter)
    gains = jnp.stack([same0, *two, *one])
    vmem, anywhere = pl.BlockSpec(memory_space=pltpu.VMEM), pl.BlockSpec(memory_space=pl.ANY)
    table = pltpu.VMEM((width, width), jnp.bfloat16)
    piece = pltpu.VMEM((chunks, parts, per, rows, quarter), jnp.float32)
    lines = 4 * per * rows
    out = pl.pallas_call(
        functools.partial(circle_kernel, bands, parts, chunks),
        out_shape=jax.ShapeDtypeStruct(state.shape, jnp.float32),
        in_specs=[vmem, vmem, vmem, anywhere],
        out_specs=anywhere,
        scratch_shapes=[
            piece,
            piece,
            table,
            table,
            pltpu.VMEM((2 * lines, width), jnp.bfloat16),
            pltpu.VMEM((lines, width), jnp.float32),
            pltpu.SemaphoreType.DMA((chunks, 2 * parts)),
            pltpu.SemaphoreType.DMA((chunks, parts)),
            pltpu.SemaphoreType.DMA((chunks, parts)),
            pltpu.SemaphoreType.DMA((chunks, 2 * parts)),
            pltpu.SemaphoreType.DMA((3,)),
        ],
        compiler_params=pltpu.CompilerParams(
            collective_id=0, has_side_effects=True, vmem_limit_bytes=50 * 2**20
        ),
    )(state, gains, twists, tables)
    return out.reshape(work_block.shape)


def per_device(model_state, courant, cutoff):
    rows_here = model_state.shape[2]
    band_index = lax.axis_index("lat")
    extended = with_halo(model_state, (("lon", 3), ("lat", 2)), 1)
    extended = trim_rims(extended, 2)
    wind_east = extended[0]
    wind_north = extended[1]
    theta_ext = extended[2]
    thickness = extended[3]
    row_courant = courant[None, :, None]
    east_flux = wind_east * thickness
    north_flux = wind_north * thickness
    heat_content = theta_ext * thickness
    new_thickness = (
        thickness[:, 1:-1, 1:-1]
        - row_courant * along_lon(east_flux)
        - meridional_courant * along_lat(north_flux)
    )
    new_heat = (
        heat_content[:, 1:-1, 1:-1]
        - row_courant * along_lon(east_flux * theta_ext)
        - meridional_courant * along_lat(north_flux * theta_ext)
    )
    new_theta = new_heat / new_thickness
    heat_ext = trim_rims(with_halo(new_heat, (("lon", 2), ("lat", 1)), 1), 1)
    new_east = wind_east[:, 1:-1, 1:-1] - pressure_gain * row_courant * along_lon(heat_ext)
    new_north = wind_north[:, 1:-1, 1:-1] - pressure_gain * meridional_courant * along_lat(heat_ext)
    stacked = jnp.stack([new_east, new_north, new_theta, new_thickness])
    parts, bands = lax.axis_size("lon"), lax.axis_size("lat")
    planes = stacked.shape[0] * stacked.shape[1]
    if parts == 4 and bands % 4 == 0 and planes % (4 * parts) == 0 and rows_here % 16 == 0:
        return shared_filter(stacked, cutoff)
    own_cut = lax.dynamic_slice_in_dim(cutoff, band_index * rows_here, rows_here)
    return filter_block(stacked, own_cut)


def solution(mesh):
    placed = (P(None, None, "lat", "lon"), P("lat"), P())
    return jax.shard_map(
        per_device,
        mesh=mesh,
        in_specs=placed,
        out_specs=P(None, None, "lat", "lon"),
        check_vma=False,
    )
```

profile of v0, /device:TPU:0, one launch (start us, length us, event | category | flops | bytes accessed | tf_op | source)
XLA Modules:
  0.0 196.9 jit_solution(1322564678522297007)
XLA Ops:
  0.0 6.4 %copy.6 = f32[4,8,32,1440]{3,1,2,0:T(8,128)S(1)} copy(f32[4,8,32,1440]{3,2,1,0:T(8,128)} %param.5) | data formatting | bytes 11796480 | tf_op args[0]
  6.4 0.0 copy-start.1
  6.4 2.7 %copy-done.1 = f32[4,8,32,1440]{3,1,2,0:T(8,128)} copy-done((f32[4,8,32,1440]{3,1,2,0:T(8,128)}, f32[4,8,32,1440]{3,1,2,0:T(8,128)S(1)}, u32[]{:S(2)}) %copy-start.1) | copy-done | bytes 5898264
  9.1 0.0 copy-start.6
  9.1 0.2 fusion.44
  9.3 0.5 collective-permute-start
  9.8 2.0 %collective-permute-start.1 = (f32[4,8,32,1]{3,1,2,0:T(8,128)S(1)}, f32[4,8,32,1]{3,1,2,0:T(8,128)S(1)}, u32[]{:S(2)}, u32[]{:S(2)}) collective-permute-start(f32[4,8,32,1]{3,1,2,0:T(8,128)S(1)} %get-tuple-element.20), channel_id=1, source_target_pairs={{8,0},{16,8},{24,16},{0,24},{9,1},{17,9},{25,17},{1,25},{10,2},{18... | collective-permute-start | bytes 12296 | tf_op jit(solution)/shard_map/ppermute | solution.py:24
  11.9 0.0 copy-done.6
  11.9 0.1 dynamic-slice_convert_fusion
  12.0 0.1 fusion.21
  12.1 0.1 multiply_dynamic-update-slice_fusion.3
  12.2 0.1 multiply_dynamic-update-slice_fusion.2
  12.3 0.0 copy-start.7
  12.3 9.3 %collective-permute-done = f32[4,8,32,1]{3,1,2,0:T(8,128)S(1)} collective-permute-done((f32[4,8,32,1]{3,1,2,0:T(8,128)S(1)}, f32[4,8,32,1]{3,1,2,0:T(8,128)S(1)}, u32[]{:S(2)}, u32[]{:S(2)}) %collective-permute-start) | collective-permute-done | bytes 4128 | tf_op jit(solution)/shard_map/ppermute | solution.py:23
  21.6 2.5 %collective-permute-done.1 = f32[4,8,32,1]{3,1,2,0:T(8,128)S(1)} collective-permute-done((f32[4,8,32,1]{3,1,2,0:T(8,128)S(1)}, f32[4,8,32,1]{3,1,2,0:T(8,128)S(1)}, u32[]{:S(2)}, u32[]{:S(2)}) %collective-permute-start.1) | collective-permute-done | bytes 4128 | tf_op jit(solution)/shard_map/ppermute | solution.py:24
  24.1 8.6 %concatenate.12 = f32[4,8,32,1442]{3,1,2,0:T(8,128)} concatenate(f32[4,8,32,1]{3,1,2,0:T(8,128)S(1)} %collective-permute-done, f32[4,8,32,1440]{3,1,2,0:T(8,128)} %copy-done.1, f32[4,8,32,1]{3,1,2,0:T(8,128)S(1)} %collective-permute-done.1), dimensions={3} | concatenate | bytes 11812864 | tf_op jit(solution)/shard_map/concatenate | solution.py:25
  32.7 1.0 fusion.43
  33.7 1.6 collective-permute-start.2
  35.3 3.2 %collective-permute-start.3 = (f32[4,8,1,1442]{3,1,2,0:T(8,128)S(1)}, f32[4,8,1,1442]{3,1,2,0:T(8,128)S(1)}, u32[]{:S(2)}, u32[]{:S(2)}) collective-permute-start(f32[4,8,1,1442]{3,1,2,0:T(8,128)S(1)} %get-tuple-element.19), channel_id=1, source_target_pairs={{1,0},{2,1},{3,2},{4,3},{5,4},{6,5},{7,6},{0,7},{9,8},{10,9},{11,1... | collective-permute-start | bytes 553736 | tf_op jit(solution)/shard_map/ppermute | solution.py:24
  38.5 0.0 copy-done.7
  38.5 6.2 %collective-permute-done.2 = f32[4,8,1,1442]{3,1,2,0:T(8,128)S(1)} collective-permute-done((f32[4,8,1,1442]{3,1,2,0:T(8,128)S(1)}, f32[4,8,1,1442]{3,1,2,0:T(8,128)S(1)}, u32[]{:S(2)}, u32[]{:S(2)}) %collective-permute-start.2) | collective-permute-done | bytes 184608 | tf_op jit(solution)/shard_map/ppermute | solution.py:23
  44.6 2.2 %collective-permute-done.3 = f32[4,8,1,1442]{3,1,2,0:T(8,128)S(1)} collective-permute-done((f32[4,8,1,1442]{3,1,2,0:T(8,128)S(1)}, f32[4,8,1,1442]{3,1,2,0:T(8,128)S(1)}, u32[]{:S(2)}, u32[]{:S(2)}) %collective-permute-start.3) | collective-permute-done | bytes 184608 | tf_op jit(solution)/shard_map/ppermute | solution.py:24
  46.8 3.6 %maximum_multiply_fusion = f32[4,8,34,1442]{3,1,2,0:T(8,128)S(1)} fusion(f32[4,8,1,1442]{3,1,2,0:T(8,128)S(1)} %collective-permute-done.3, f32[4,8,32,1442]{3,1,2,0:T(8,128)} %concatenate.12, f32[4,8,1,1442]{3,1,2,0:T(8,128)S(1)} %collective-permute-done.2, f32[34]{0:T(128)S(1)} %not_convert_fusion), kind=kLoop, calls=%fused_computation | loop fusion | flops 4706688 | bytes 12551304 | tf_op jit(solution)/shard_map/mul | solution.py:140
  50.5 2.4 %slice_bitcast_fusion.3 = (f32[8,34,1442]{2,0,1:T(8,128)}, f32[8,34,1442]{2,0,1:T(8,128)}, f32[8,34,1442]{2,0,1:T(8,128)S(1)}, f32[8,34,1442]{2,0,1:T(8,128)S(1)}) fusion(f32[4,8,34,1442]{3,1,2,0:T(8,128)S(1)} %maximum_multiply_fusion), kind=kLoop, calls=%fused_computation.5 | loop fusion | bytes 12551168 | tf_op jit(solution)/shard_map/squeeze | solution.py:452
  52.9 1.0 fusion.38
  53.9 4.6 %divide_bitcast_fusion = (f32[1,8,32,1440]{3,1,2,0:T(8,128)}, f32[8,32,1440]{2,0,1:T(8,128)S(1)}, f32[8,32,1440]{2,0,1:T(8,128)}) fusion(f32[8,34,1442]{2,0,1:T(8,128)S(1)} %get-tuple-element.16, f32[32]{0:T(128)S(1)} %get-tuple-element.29, f32[8,34,1442]{2,0,1:T(8,128)S(1)} %get-tuple-element.8, f32[8,34,1442]{2,0,1:T(8,128)S(1)} %get-tuple-element.14, ...), kind=kLoop, calls=%fused_computation.28 | loop fusion | flops 5160960 | bytes 19169408 | tf_op jit(solution)/shard_map/stack | solution.py:474
  58.5 0.1 fusion.46
  58.6 0.1 collective-permute-start.4
  58.7 1.7 collective-permute-start.5
  60.4 0.1 multiply_dynamic-update-slice_fusion.1
  60.5 2.5 %collective-permute-done.4 = f32[8,32,1]{2,0,1:T(8,128)S(1)} collective-permute-done((f32[8,32,1]{2,0,1:T(8,128)S(1)}, f32[8,32,1]{2,0,1:T(8,128)S(1)}, u32[]{:S(2)}, u32[]{:S(2)}) %collective-permute-start.4) | collective-permute-done | bytes 1056 | tf_op jit(solution)/shard_map/ppermute | solution.py:23
  63.1 0.4 collective-permute-done.5
  63.5 1.6 concatenate.14
  65.1 0.8 fusion.45
  65.9 0.3 collective-permute-start.6
  66.3 4.4 %collective-permute-start.7 = (f32[8,1,1442]{2,0,1:T(8,128)S(1)}, f32[8,1,1442]{2,0,1:T(8,128)S(1)}, u32[]{:S(2)}, u32[]{:S(2)}) collective-permute-start(f32[8,1,1442]{2,0,1:T(8,128)S(1)} %get-tuple-element.25), channel_id=1, source_target_pairs={{1,0},{2,1},{3,2},{4,3},{5,4},{6,5},{7,6},{0,7},{9,8},{10,9},{11,1... | collective-permute-start | bytes 138440 | tf_op jit(solution)/shard_map/ppermute | solution.py:24
  70.7 0.1 multiply_dynamic-update-slice_fusion.gains
  70.8 0.0 copy-start.2
  70.8 0.0 copy-start.3
  70.8 2.2 %collective-permute-done.6 = f32[8,1,1442]{2,0,1:T(8,128)S(1)} collective-permute-done((f32[8,1,1442]{2,0,1:T(8,128)S(1)}, f32[8,1,1442]{2,0,1:T(8,128)S(1)}, u32[]{:S(2)}, u32[]{:S(2)}) %collective-permute-start.6) | collective-permute-done | bytes 46176 | tf_op jit(solution)/shard_map/ppermute | solution.py:23
  73.1 0.0 collective-permute-done.7
  73.1 1.6 maximum_multiply_fusion.1
  74.7 0.0 copy-done.2
  74.7 0.0 copy-done.3
  74.7 0.0 copy-start.4
  74.7 0.0 copy-start.5
  74.7 2.1 %fusion.9 = (f32[1,8,32,1440]{3,1,2,0:T(8,128)S(1)}, f32[1,8,32,1440]{3,1,2,0:T(8,128)S(1)}) fusion(f32[8,34,1442]{2,0,1:T(8,128)S(1)} %maximum_multiply_fusion.1, f32[8,34,1442]{2,0,1:T(8,128)S(1)} %copy-done.2, f32[32]{0:T(128)S(1)} %get-tuple-element.28, f32[8,34,1442]{2,0,1:T(8,128)S(1)} %copy-done.3), kind=kLoop, calls=%fused_computation.20 | loop fusion | flops 2211840 | bytes 11796608 | tf_op jit(solution)/shard_map/stack | solution.py:474
  76.8 0.0 copy-done.4
  76.8 0.0 copy-done.5
  76.8 0.5 pad_maximum_fusion
  77.3 0.0 copy-start
  77.3 6.3 %copy.9 = f32[4,8,32,1440]{3,2,1,0:T(8,128)} copy(f32[4,8,32,1440]{3,1,2,0:T(8,128)S(1)} %pad_maximum_fusion) | data formatting | bytes 11796480 | tf_op jit(solution)/shard_map/stack | solution.py:474
  83.7 0.0 copy-done
  83.7 107.0 %shard_map.55 = f32[32,32,1440]{2,1,0:T(8,128)} custom-call(f32[32,32,1440]{2,1,0:T(8,128)} %bitcast.33, f32[5,32,768]{2,1,0:T(8,128)S(1)} %multiply_dynamic-update-slice_fusion.gains, f32[4,1440]{1,0:T(4,128)S(1)} %copy-done, bf16[2,1536,1536]{2,1,0:T(8,128)(2,1)} %constant.65.clone.tables), custom_call_target="tpu_custom_call" | custom-call | tf_op jit(solution)/shard_map/pallas_call | solution.py:422
  190.7 6.2 %copy.15 = f32[4,8,32,1440]{3,2,1,0:T(8,128)} copy(f32[4,8,32,1440]{3,2,1,0:T(8,128)} %bitcast.34) | data formatting | bytes 11796480
  (7 shorter events, 0.1 us)
Async XLA Ops:
  6.4 2.7 %copy-start.1 = (f32[4,8,32,1440]{3,1,2,0:T(8,128)}, f32[4,8,32,1440]{3,1,2,0:T(8,128)S(1)}, u32[]{:S(2)}) copy-start(f32[4,8,32,1440]{3,1,2,0:T(8,128)S(1)} %copy.6) | copy-start | bytes 17694724
  9.1 2.8 %copy-start.6 = (s32[256]{0:T(256)S(1)}, s32[256]{0:T(256)}, u32[]{:S(2)}) copy-start(s32[256]{0:T(256)} %param.7) | copy-start | bytes 3076
  9.3 12.2 %collective-permute-start = (f32[4,8,32,1]{3,1,2,0:T(8,128)S(1)}, f32[4,8,32,1]{3,1,2,0:T(8,128)S(1)}, u32[]{:S(2)}, u32[]{:S(2)}) collective-permute-start(f32[4,8,32,1]{3,1,2,0:T(8,128)S(1)} %get-tuple-element.21), channel_id=1, source_target_pairs={{0,8},{8,16},{16,24},{24,0},{1,9},{9,17},{17,25},{25,1},{2,10},{10... | collective-permute-start | bytes 12296 | tf_op jit(solution)/shard_map/ppermute | solution.py:23
  9.8 14.2 %collective-permute-start.1 = (f32[4,8,32,1]{3,1,2,0:T(8,128)S(1)}, f32[4,8,32,1]{3,1,2,0:T(8,128)S(1)}, u32[]{:S(2)}, u32[]{:S(2)}) collective-permute-start(f32[4,8,32,1]{3,1,2,0:T(8,128)S(1)} %get-tuple-element.20), channel_id=1, source_target_pairs={{8,0},{16,8},{24,16},{0,24},{9,1},{17,9},{25,17},{1,25},{10,2},{18... | collective-permute-start | bytes 12296 | tf_op jit(solution)/shard_map/ppermute | solution.py:24
  12.3 26.2 %copy-start.7 = (f32[32]{0:T(128)S(1)}, f32[32]{0:T(128)}, u32[]{:S(2)}) copy-start(f32[32]{0:T(128)} %param.6) | copy-start | bytes 388
  33.7 10.9 %collective-permute-start.2 = (f32[4,8,1,1442]{3,1,2,0:T(8,128)S(1)}, f32[4,8,1,1442]{3,1,2,0:T(8,128)S(1)}, u32[]{:S(2)}, u32[]{:S(2)}) collective-permute-start(f32[4,8,1,1442]{3,1,2,0:T(8,128)S(1)} %get-tuple-element.18), channel_id=1, source_target_pairs={{0,1},{1,2},{2,3},{3,4},{4,5},{5,6},{6,7},{7,0},{8,9},{9,10},{10,1... | collective-permute-start | bytes 553736 | tf_op jit(solution)/shard_map/ppermute | solution.py:23
  35.3 11.6 %collective-permute-start.3 = (f32[4,8,1,1442]{3,1,2,0:T(8,128)S(1)}, f32[4,8,1,1442]{3,1,2,0:T(8,128)S(1)}, u32[]{:S(2)}, u32[]{:S(2)}) collective-permute-start(f32[4,8,1,1442]{3,1,2,0:T(8,128)S(1)} %get-tuple-element.19), channel_id=1, source_target_pairs={{1,0},{2,1},{3,2},{4,3},{5,4},{6,5},{7,6},{0,7},{9,8},{10,9},{11,1... | collective-permute-start | bytes 553736 | tf_op jit(solution)/shard_map/ppermute | solution.py:24
  58.6 4.4 %collective-permute-start.4 = (f32[8,32,1]{2,0,1:T(8,128)S(1)}, f32[8,32,1]{2,0,1:T(8,128)S(1)}, u32[]{:S(2)}, u32[]{:S(2)}) collective-permute-start(f32[8,32,1]{2,0,1:T(8,128)S(1)} %get-tuple-element.27), channel_id=1, source_target_pairs={{0,8},{8,16},{16,24},{24,0},{1,9},{9,17},{17,25},{25,1},{2,10},{10... | collective-permute-start | bytes 3080 | tf_op jit(solution)/shard_map/ppermute | solution.py:23
  58.7 4.8 %collective-permute-start.5 = (f32[8,32,1]{2,0,1:T(8,128)S(1)}, f32[8,32,1]{2,0,1:T(8,128)S(1)}, u32[]{:S(2)}, u32[]{:S(2)}) collective-permute-start(f32[8,32,1]{2,0,1:T(8,128)S(1)} %get-tuple-element.26), channel_id=1, source_target_pairs={{8,0},{16,8},{24,16},{0,24},{9,1},{17,9},{25,17},{1,25},{10,2},{18... | collective-permute-start | bytes 3080 | tf_op jit(solution)/shard_map/ppermute | solution.py:24
  65.9 7.1 %collective-permute-start.6 = (f32[8,1,1442]{2,0,1:T(8,128)S(1)}, f32[8,1,1442]{2,0,1:T(8,128)S(1)}, u32[]{:S(2)}, u32[]{:S(2)}) collective-permute-start(f32[8,1,1442]{2,0,1:T(8,128)S(1)} %get-tuple-element.24), channel_id=1, source_target_pairs={{0,1},{1,2},{2,3},{3,4},{4,5},{5,6},{6,7},{7,0},{8,9},{9,10},{10,1... | collective-permute-start | bytes 138440 | tf_op jit(solution)/shard_map/ppermute | solution.py:23
  66.3 6.8 %collective-permute-start.7 = (f32[8,1,1442]{2,0,1:T(8,128)S(1)}, f32[8,1,1442]{2,0,1:T(8,128)S(1)}, u32[]{:S(2)}, u32[]{:S(2)}) collective-permute-start(f32[8,1,1442]{2,0,1:T(8,128)S(1)} %get-tuple-element.25), channel_id=1, source_target_pairs={{1,0},{2,1},{3,2},{4,3},{5,4},{6,5},{7,6},{0,7},{9,8},{10,9},{11,1... | collective-permute-start | bytes 138440 | tf_op jit(solution)/shard_map/ppermute | solution.py:24
  70.8 3.9 %copy-start.2 = (f32[8,34,1442]{2,0,1:T(8,128)S(1)}, f32[8,34,1442]{2,0,1:T(8,128)}, u32[]{:S(2)}) copy-start(f32[8,34,1442]{2,0,1:T(8,128)} %get-tuple-element.12) | copy-start | bytes 4706692
  70.8 3.9 %copy-start.3 = (f32[8,34,1442]{2,0,1:T(8,128)S(1)}, f32[8,34,1442]{2,0,1:T(8,128)}, u32[]{:S(2)}) copy-start(f32[8,34,1442]{2,0,1:T(8,128)} %get-tuple-element.13) | copy-start | bytes 4706692
  74.7 2.1 %copy-start.4 = (f32[1,8,32,1440]{3,1,2,0:T(8,128)S(1)}, f32[1,8,32,1440]{3,1,2,0:T(8,128)}, u32[]{:S(2)}) copy-start(f32[1,8,32,1440]{3,1,2,0:T(8,128)} %get-tuple-element.5) | copy-start | bytes 4423684
  74.7 2.1 %copy-start.5 = (f32[8,32,1440]{2,0,1:T(8,128)S(1)}, f32[8,32,1440]{2,0,1:T(8,128)}, u32[]{:S(2)}) copy-start(f32[8,32,1440]{2,0,1:T(8,128)} %get-tuple-element.7) | copy-start | bytes 4423684
  77.3 6.4 %copy-start = (f32[4,1440]{1,0:T(4,128)S(1)}, f32[4,1440]{1,0:T(4,128)}, u32[]{:S(2)}) copy-start(f32[4,1440]{1,0:T(4,128)} %constant.66.clone.twists) | copy-start | bytes 69124
where the time goes:
time: 198 us; the launch traced here: 197 us
  Pallas kernels  107 us (54%)
  local copies, waits for them, and re-layouts  36.5 us (18%)
  waiting for transfers between devices  25.3 us (13%)
  other arithmetic  14 us (7%)
  starting transfers between devices  13.8 us (7%)
    pallas_call x1, Pallas kernels, shared_filter(): pl.pallas_call(functools.partial(circle_kernel, bands, parts, chunks), ou...  107 us
    ppermute x4, waiting for transfers between devices, with_halo(): before = lax.ppermute(last, axis, up)  20.2 us
    unnamed x18, local copies, waits for them, and re-layouts  15.4 us
    ppermute x4, starting transfers between devices, with_halo(): after = lax.ppermute(first, axis, down)  11.4 us
    concatenate x2, local copies, waits for them, and re-layouts, with_halo(): array = jnp.concatenate([before, array, after], axis=dim)  10.2 us
    another operation x3, other arithmetic, per_device(): stacked = jnp.stack([new_east, new_north, new_theta, new_thickness])  7.19 us
    another operation x1, local copies, waits for them, and re-layouts, per_device(): stacked = jnp.stack([new_east, new_north, new_theta, new_thickness])  6.35 us
    mul x2, other arithmetic, trim_rims(): return extended * keep_rows.astype(extended.dtype).reshape(mask_shape)  5.18 us
  transfers between devices with their start and end apart: 8, of which 7 were waited for; matrix products, arithmetic and copies ran while one was open for 0% of the time, Pallas kernels for 0%

commit v1 on v0

--- a/solution.py
+++ b/solution.py
@@ -10,6 +10,7 @@
 
 meridional_courant = 0.05
 pressure_gain = 4.0
+courant_lane = 64
 MESH = pl.DeviceIdType.MESH
 
 
@@ -195,87 +196,217 @@
         out_ref[:, cols] = (both[:rows] + both[rows:]) + cross
 
 
+def edge_tile(state, ring, courant, component, level, rows):
+    rest = state.shape[3] % 128
+    tail = state[component, level, rows, state.shape[3] - rest :]
+    count = tail.shape[0]
+    tail = jnp.concatenate([tail, jnp.zeros((count, 128 - rest), jnp.float32)], axis=1)
+    lane = lax.broadcasted_iota(jnp.int32, (count, 128), 1)
+    tile = jnp.where(lane == courant_lane, courant[rows, :], tail)
+    tile = jnp.where((lane == rest) | (lane == rest + 1), ring[1, component, level, rows, :], tile)
+    return jnp.where(lane >= 126, ring[0, component, level, rows, :], tile)
+
+
+def substep_level(state, ring, caps, courant, field, work, level, first, last):
+    components, levels, rows, quarter = state.shape
+    width = field.shape[2]
+    body = width - 128
+    for c in range(components):
+        field[c, 8 : 8 + rows, :body] = state[c, level, :, :body]
+        field[c, 8 : 8 + rows, body:] = edge_tile(state, ring, courant, c, level, slice(0, rows))
+        field[c, 6:8, :] = caps[0, 2 * (c * levels + level) : 2 * (c * levels + level) + 2, :]
+        field[c, 8 + rows : 10 + rows, :] = caps[1, 2 * (c * levels + level) : 2 * (c * levels + level) + 2, :]
+    east, north, theta, thick = (field[c] for c in range(4))
+    height = east.shape[0]
+    row_courant = east[:, body + courant_lane : body + courant_lane + 1]
+
+    def along_x(f):
+        return (pltpu.roll(f, width - 1, 1) - pltpu.roll(f, 1, 1)) * 0.5
+
+    def along_y(f):
+        return (pltpu.roll(f, height - 1, 0) - pltpu.roll(f, 1, 0)) * 0.5
+
+    east_flux, north_flux = east * thick, north * thick
+    new_thick = thick - row_courant * along_x(east_flux) - meridional_courant * along_y(north_flux)
+    heat = (
+        theta * thick
+        - row_courant * along_x(east_flux * theta)
+        - meridional_courant * along_y(north_flux * theta)
+    )
+    row = lax.broadcasted_iota(jnp.int32, (height, 1), 0)
+    beyond = (first & (row < 8)) | (last & (row >= 8 + rows))
+    heat = jnp.where(beyond, 0.0, heat)
+    new_east = east - pressure_gain * row_courant * along_x(heat)
+    new_north = north - pressure_gain * meridional_courant * along_y(heat)
+    own = slice(8, 8 + rows)
+    work[0, level] = new_east[own, :quarter]
+    work[1, level] = new_north[own, :quarter]
+    work[2, level] = heat[own, :quarter] / new_thick[own, :quarter]
+    work[3, level] = new_thick[own, :quarter]
+
+
 def circle_kernel(
-    bands, parts, chunks, state, gains, twists, tables, out, circles, results, high, low, operand, waves,
-    send_sem, recv_sem, back_send_sem, back_recv_sem, local_sem,
+    bands, parts, chunks, state, courant, gains, twists, table, out, circles, results, basis, high, low,
+    operand, waves, pack, ring, edges, caps, field, work,
+    send_sem, recv_sem, back_send_sem, back_recv_sem, local_sem, halo_send, halo_recv,
 ):
     part = lax.axis_index("lon")
     band = lax.axis_index("lat")
     polar, source, helper = worker_group(band, bands)
     _, _, per, rows, quarter = circles.shape
+    components, levels, rows_here, _ = state.shape
     width = high.shape[1]
     lanes = width // 2
-    workers = 2 * parts
-    row_chunks = state.shape[1] // rows
-    planes_per = state.shape[0] // workers
+    row_chunks = rows_here // rows
     me = jnp.where(polar, part, part + parts)
+    first, last = band == 0, band == bands - 1
 
     def block(ref, worker, chunk):
-        plane = worker * planes_per + (chunk // row_chunks) * per
+        level = (chunk // row_chunks) * 2 * per + (worker // parts) * per
         row = pl.multiple_of((chunk % row_chunks) * rows, rows)
-        return ref.at[pl.ds(plane, per), pl.ds(row, rows), :]
-
+        return ref.at[lax.rem(worker, parts), pl.ds(level, per), pl.ds(row, rows), :]
+
+    load = pltpu.make_async_copy(table, basis, local_sem.at[0])
+    load.start()
+
+    caps[...] = jnp.zeros_like(caps)
     barrier = pltpu.get_barrier_semaphore()
+
+    def greet(there, row_band):
+        pl.semaphore_signal(barrier, inc=1, device_id=(there, row_band), device_id_type=MESH)
+
     for step in range(1, parts):
+        greet(lax.rem(part + step, parts), band)
+    for step in range(parts):
+        greet(lax.rem(part + step, parts), jnp.where(polar, helper, source))
+
+    @pl.when(band > 0)
+    def _():
+        greet(part, band - 1)
+
+    @pl.when(band < bands - 1)
+    def _():
+        greet(part, band + 1)
+
+    rest = quarter % 128
+    lane = lax.broadcasted_iota(jnp.int32, (rows_here, 128), 1)
+
+    @pl.loop(0, levels)
+    def _(level):
+        for c in range(components):
+            begin = pltpu.roll(state[c, level, :, :128], rest, 1)
+            tail = state[c, level, :, quarter - rest :]
+            tail = jnp.concatenate([tail, jnp.zeros((rows_here, 128 - rest), jnp.float32)], axis=1)
+            pack[c, level] = jnp.where(lane >= 126, pltpu.roll(tail, 128 - rest, 1), begin)
+
+    inner_bands = jnp.where(first | last, 1, 2)
+    pl.semaphore_wait(barrier, 2 * parts - 1 + inner_bands)
+    columns = [
+        pltpu.make_async_remote_copy(
+            src_ref=pack,
+            dst_ref=ring.at[slot],
+            send_sem=halo_send.at[slot],
+            recv_sem=halo_recv.at[slot],
+            device_id=(lax.rem(part + shift, parts), band),
+            device_id_type=MESH,
+        )
+        for slot, shift in ((0, 1), (1, parts - 1))
+    ]
+    for copy in columns:
+        copy.start()
+    field[...] = jnp.zeros_like(field)
+    operand[...] = jnp.zeros_like(operand)
+    load.wait()
+
+    @pl.loop(0, width // 32)
+    def _(step):
+        at = pl.ds(pl.multiple_of(step * 32, 32), 32)
+        exact = basis[at, :]
+        upper = exact.astype(jnp.bfloat16)
+        high[at, :] = upper
+        low[at, :] = (exact - upper.astype(jnp.float32)).astype(jnp.bfloat16)
+
+    for copy in columns:
+        copy.wait()
+
+    body = width - 128
+    for c in range(components):
+        for level in range(levels):
+            at = slice(2 * (c * levels + level), 2 * (c * levels + level) + 2)
+            for slot, own in ((0, slice(rows_here - 2, rows_here)), (1, slice(0, 2))):
+                edges[slot, at, :body] = state[c, level, own, :body]
+                edges[slot, at, body:] = edge_tile(state, ring, courant, c, level, own)
+
+    def rows_to(slot, row_band):
+        return pltpu.make_async_remote_copy(
+            src_ref=edges.at[slot],
+            dst_ref=caps.at[slot],
+            send_sem=halo_send.at[2 + slot],
+            recv_sem=halo_recv.at[2 + slot],
+            device_id=(part, row_band),
+            device_id_type=MESH,
+        )
+
+    @pl.when(jnp.logical_not(last))
+    def _():
+        rows_to(0, band + 1).start()
+
+    @pl.when(jnp.logical_not(first))
+    def _():
+        rows_to(1, band - 1).start()
+
+    @pl.when(jnp.logical_not(first))
+    def _():
+        rows_to(1, band - 1).wait_send()
+        pltpu.make_async_copy(caps.at[0], caps.at[0], halo_recv.at[2]).wait()
+
+    @pl.when(jnp.logical_not(last))
+    def _():
+        rows_to(0, band + 1).wait_send()
+        pltpu.make_async_copy(caps.at[1], caps.at[1], halo_recv.at[3]).wait()
+
+    through = pltpu.make_async_copy(work, out, local_sem.at[1])
+
+    def send_chunk(chunk):
+        for step in range(parts):
+            there = lax.rem(part + step, parts)
+            pltpu.make_async_remote_copy(
+                src_ref=block(work, there + parts, chunk),
+                dst_ref=circles.at[chunk, part],
+                send_sem=send_sem.at[chunk, there + parts],
+                recv_sem=recv_sem.at[chunk, part],
+                device_id=(there, helper),
+                device_id_type=MESH,
+            ).start()
+            if step == 0:
+                pltpu.make_async_copy(
+                    block(work, me, chunk), circles.at[chunk, part], recv_sem.at[chunk, part]
+                ).start()
+            else:
+                pltpu.make_async_remote_copy(
+                    src_ref=block(work, there, chunk),
+                    dst_ref=circles.at[chunk, part],
+                    send_sem=send_sem.at[chunk, there],
+                    recv_sem=recv_sem.at[chunk, part],
+                    device_id=(there, band),
+                    device_id_type=MESH,
+                ).start()
+
+    span = 2 * per
+    for begin in range(0, levels, span):
+        for level in range(begin, begin + span):
+            substep_level(state, ring, caps, courant, field, work, level, first, last)
+
         @pl.when(polar)
         def _():
-            pl.semaphore_signal(
-                barrier, inc=1, device_id=(lax.rem(part + step, parts), band), device_id_type=MESH
-            )
-    for step in range(parts):
-        pl.semaphore_signal(
-            barrier,
-            inc=1,
-            device_id=(lax.rem(part + step, parts), jnp.where(polar, helper, source)),
-            device_id_type=MESH,
-        )
-
-    loads = [
-        pltpu.make_async_copy(tables.at[i], ref, local_sem.at[i])
-        for i, ref in enumerate((high, low))
-    ]
-    for load in loads:
-        load.start()
-    through = pltpu.make_async_copy(state, out, local_sem.at[2])
+            @pl.loop(begin // span * row_chunks, (begin // span + 1) * row_chunks)
+            def _(chunk):
+                send_chunk(chunk)
 
     @pl.when(jnp.logical_not(polar))
     def _():
         through.start()
-        pl.semaphore_wait(barrier, parts)
-
-    @pl.when(polar)
-    def _():
-        pl.semaphore_wait(barrier, 2 * parts - 1)
-
-        @pl.loop(0, chunks)
-        def _(chunk):
-            for step in range(parts):
-                there = lax.rem(part + step, parts)
-                pltpu.make_async_remote_copy(
-                    src_ref=block(state, there + parts, chunk),
-                    dst_ref=circles.at[chunk, part],
-                    send_sem=send_sem.at[chunk, there + parts],
-                    recv_sem=recv_sem.at[chunk, part],
-                    device_id=(there, helper),
-                    device_id_type=MESH,
-                ).start()
-                if step == 0:
-                    pltpu.make_async_copy(
-                        block(state, me, chunk), circles.at[chunk, part], recv_sem.at[chunk, part]
-                    ).start()
-                else:
-                    pltpu.make_async_remote_copy(
-                        src_ref=block(state, there, chunk),
-                        dst_ref=circles.at[chunk, part],
-                        send_sem=send_sem.at[chunk, there],
-                        recv_sem=recv_sem.at[chunk, part],
-                        device_id=(there, band),
-                        device_id_type=MESH,
-                    ).start()
-
-    operand[...] = jnp.zeros_like(operand)
-    for load in loads:
-        load.wait()
+
     cos1, sin1, cos2, sin2 = (twists[i : i + 1, :] for i in range(4))
     half, whole = rows, per * rows
 
@@ -385,30 +516,26 @@
         def _():
             for step in range(parts):
                 there = lax.rem(part + step, parts)
-                drain(block(state, there + parts, chunk), send_sem.at[chunk, there + parts])
+                drain(block(work, there + parts, chunk), send_sem.at[chunk, there + parts])
                 drain(block(out, there + parts, chunk), back_recv_sem.at[chunk, there + parts])
                 drain(block(out, there, chunk), back_recv_sem.at[chunk, there])
                 if step > 0:
-                    drain(block(state, there, chunk), send_sem.at[chunk, there])
+                    drain(block(work, there, chunk), send_sem.at[chunk, there])
 
     @pl.when(jnp.logical_not(polar))
     def _():
         through.wait()
 
 
-def shared_filter(work_block, cutoff):
+def shared_substep(state, courant, cutoff):
     parts, bands = lax.axis_size("lon"), lax.axis_size("lat")
-    components, levels, rows_here, quarter = work_block.shape
-    state = work_block.reshape(components * levels, rows_here, quarter)
+    components, levels, rows_here, quarter = state.shape
     per, rows = 2, 16
     chunks = (components * levels // (2 * parts) // per) * (rows_here // rows)
     basis = quarter_basis(quarter)
     width = basis.shape[1]
     square = np.zeros((width, width), np.float32)
     square[:quarter] = basis
-    high = square.astype(jnp.bfloat16)
-    low = (square - high.astype(np.float32)).astype(jnp.bfloat16)
-    tables = jnp.asarray(np.stack([high, low]))
     cos_twist, sin_twist = quarter_twists(quarter)
     twists = jnp.asarray(np.stack([cos_twist[0], sin_twist[0], cos_twist[1], sin_twist[1]]))
     _, source, _ = worker_group(lax.axis_index("lat"), bands)
@@ -419,32 +546,56 @@
     table = pltpu.VMEM((width, width), jnp.bfloat16)
     piece = pltpu.VMEM((chunks, parts, per, rows, quarter), jnp.float32)
     lines = 4 * per * rows
-    out = pl.pallas_call(
+    pairs = 2 * components * levels
+    return pl.pallas_call(
         functools.partial(circle_kernel, bands, parts, chunks),
         out_shape=jax.ShapeDtypeStruct(state.shape, jnp.float32),
-        in_specs=[vmem, vmem, vmem, anywhere],
+        in_specs=[vmem, vmem, vmem, vmem, anywhere],
         out_specs=anywhere,
         scratch_shapes=[
             piece,
             piece,
+            pltpu.VMEM((width, width), jnp.float32),
             table,
             table,
             pltpu.VMEM((2 * lines, width), jnp.bfloat16),
             pltpu.VMEM((lines, width), jnp.float32),
+            pltpu.VMEM((components, levels, rows_here, 128), jnp.float32),
+            pltpu.VMEM((2, components, levels, rows_here, 128), jnp.float32),
+            pltpu.VMEM((2, pairs, width), jnp.float32),
+            pltpu.VMEM((2, pairs, width), jnp.float32),
+            pltpu.VMEM((components, rows_here + 16, width), jnp.float32),
+            pltpu.VMEM(state.shape, jnp.float32),
             pltpu.SemaphoreType.DMA((chunks, 2 * parts)),
             pltpu.SemaphoreType.DMA((chunks, parts)),
             pltpu.SemaphoreType.DMA((chunks, parts)),
             pltpu.SemaphoreType.DMA((chunks, 2 * parts)),
-            pltpu.SemaphoreType.DMA((3,)),
+            pltpu.SemaphoreType.DMA((2,)),
+            pltpu.SemaphoreType.DMA((4,)),
+            pltpu.SemaphoreType.DMA((4,)),
         ],
         compiler_params=pltpu.CompilerParams(
-            collective_id=0, has_side_effects=True, vmem_limit_bytes=50 * 2**20
+            collective_id=0, has_side_effects=True, vmem_limit_bytes=56 * 2**20
         ),
-    )(state, gains, twists, tables)
-    return out.reshape(work_block.shape)
+    )(state, courant[:, None], gains, twists, jnp.asarray(square))
+
+
+def fits_shared(state):
+    parts, bands = lax.axis_size("lon"), lax.axis_size("lat")
+    components, levels, rows_here, quarter = state.shape
+    return (
+        parts == 4
+        and components == parts
+        and bands % 4 == 0
+        and levels % 4 == 0
+        and rows_here % 16 == 0
+        and quarter % 128 == 32
+    )
 
 
 def per_device(model_state, courant, cutoff):
+    if fits_shared(model_state):
+        return shared_substep(model_state, courant, cutoff)
     rows_here = model_state.shape[2]
     band_index = lax.axis_index("lat")
     extended = with_halo(model_state, (("lon", 3), ("lat", 2)), 1)
@@ -472,10 +623,6 @@
     new_east = wind_east[:, 1:-1, 1:-1] - pressure_gain * row_courant * along_lon(heat_ext)
     new_north = wind_north[:, 1:-1, 1:-1] - pressure_gain * meridional_courant * along_lat(heat_ext)
     stacked = jnp.stack([new_east, new_north, new_theta, new_thickness])
-    parts, bands = lax.axis_size("lon"), lax.axis_size("lat")
-    planes = stacked.shape[0] * stacked.shape[1]
-    if parts == 4 and bands % 4 == 0 and planes % (4 * parts) == 0 and rows_here % 16 == 0:
-        return shared_filter(stacked, cutoff)
     own_cut = lax.dynamic_slice_in_dim(cutoff, band_index * rows_here, rows_here)
     return filter_block(stacked, own_cut)
 

time: 198 us -> 154 us (0.78)
  Pallas kernels: 107 us -> 142 us
  local copies, waits for them, and re-layouts: 36.5 us -> 8.31 us
  waiting for transfers between devices: 25.3 us -> 0 us
  starting transfers between devices: 13.8 us -> 0 us
  other arithmetic: 14 us -> 1.27 us
    pallas_call x1, Pallas kernels: 107 us -> 142 us  [shared_substep(): pl.pallas_call(functools.partial(circle_kernel, bands, parts, chunks), ou...]
    ppermute x8 -> x0, waiting for transfers between devices: 25.3 us -> none  [the longest x4 20.2 us: with_halo(): before = lax.ppermute(last, axis, up)]
    ppermute x8 -> x0, starting transfers between devices: 13.8 us -> none  [the longest x4 11.4 us: with_halo(): after = lax.ppermute(first, axis, down)]
    concatenate x2 -> x0, local copies, waits for them, and re-layouts: 10.2 us -> none  [with_halo(): array = jnp.concatenate([before, array, after], axis=dim)]
    unnamed x18 -> x3, local copies, waits for them, and re-layouts: 15.4 us -> 6.98 us
    another operation x4 -> x1, other arithmetic: 7.29 us -> 0.1 us  [shared_substep(): gains = jnp.stack([same0, *two, *one])]
    another operation x1 -> x0, local copies, waits for them, and re-layouts: 6.35 us -> none  [per_device(): stacked = jnp.stack([new_east, new_north, new_theta, new_thickness])]
    mul x4 -> x0, other arithmetic: 6.2 us -> none  [the longest x2 5.18 us: trim_rims(): return extended * keep_rows.astype(extended.dtype).reshape(mask_shape)]
  transfers between devices with their start and end apart: 8 -> 0, of which waited for: 7 -> 0; matrix products, arithmetic and copies ran while one was open for 0% -> 0% of each run, Pallas kernels for 0% -> 0%
where the time goes in v1:
time: 154 us; the launch traced here: 152 us
  Pallas kernels  142 us (92%)
  local copies, waits for them, and re-layouts  8.31 us (5%)
    pallas_call x1, Pallas kernels, shared_substep(): pl.pallas_call(functools.partial(circle_kernel, bands, parts, chunks), ou...  142 us
    unnamed x3, local copies, waits for them, and re-layouts  6.98 us

profile of v1, /device:TPU:0, one launch (start us, length us, event | category | flops | bytes accessed | tf_op | source)
XLA Modules:
  0.0 152.1 jit_solution(16855562729808626418)
XLA Ops:
  0.0 0.8 dynamic-slice_convert_fusion
  0.8 1.3 copy.6.courant
  2.1 0.1 fusion.7
  2.2 0.1 multiply_dynamic-update-slice_fusion.3
  2.3 0.1 multiply_dynamic-update-slice_fusion.2
  2.4 0.1 multiply_dynamic-update-slice_fusion.1
  2.5 0.1 multiply_dynamic-update-slice_fusion.gains
  2.6 0.0 copy-start
  2.7 0.8 copy-done
  3.4 142.5 %shard_map.55 = f32[4,8,32,1440]{3,2,1,0:T(8,128)} custom-call(f32[4,8,32,1440]{3,2,1,0:T(8,128)} %state.1, f32[32,1]{1,0:T(8,128)} %copy.6.courant, f32[5,32,768]{2,1,0:T(8,128)} %copy-done, f32[4,1440]{1,0:T(4,128)} %constant.49.clone.twists, f32[1536,1536]{1,0:T(8,128)} %constant.50.clone.table), custom_call_target="tpu_custom_call" | custom-call | tf_op jit(solution)/shard_map/pallas_call | solution.py:550
  145.9 6.2 %copy.12 = f32[4,8,32,1440]{3,2,1,0:T(8,128)} copy(f32[4,8,32,1440]{3,2,1,0:T(8,128)} %shard_map.55) | data formatting | bytes 11796480
  (5 shorter events, 0.0 us)
Async XLA Ops:
  2.6 0.8 copy-start

commit v2 on v1

--- a/solution.py
+++ b/solution.py
@@ -247,8 +247,9 @@
 
 def circle_kernel(
     bands, parts, chunks, state, courant, gains, twists, table, out, circles, results, basis, high, low,
-    operand, waves, pack, ring, edges, caps, field, work,
+    operand, waves, pack, ring, edges, caps, field, work, relay,
     send_sem, recv_sem, back_send_sem, back_recv_sem, local_sem, halo_send, halo_recv,
+    relay_send, relay_recv,
 ):
     part = lax.axis_index("lon")
     band = lax.axis_index("lat")
@@ -367,30 +368,28 @@
 
     through = pltpu.make_async_copy(work, out, local_sem.at[1])
 
+    sibling = part + 1 - 2 * lax.rem(part, 2)
+    far = (lax.rem(part + 2, parts), lax.rem(sibling + 2, parts))
+
     def send_chunk(chunk):
-        for step in range(parts):
-            there = lax.rem(part + step, parts)
+        def send(worker, target, target_band, slot, semaphore):
             pltpu.make_async_remote_copy(
-                src_ref=block(work, there + parts, chunk),
-                dst_ref=circles.at[chunk, part],
-                send_sem=send_sem.at[chunk, there + parts],
-                recv_sem=recv_sem.at[chunk, part],
-                device_id=(there, helper),
+                src_ref=block(work, worker, chunk),
+                dst_ref=slot,
+                send_sem=send_sem.at[chunk, worker],
+                recv_sem=semaphore,
+                device_id=(target, target_band),
                 device_id_type=MESH,
             ).start()
-            if step == 0:
-                pltpu.make_async_copy(
-                    block(work, me, chunk), circles.at[chunk, part], recv_sem.at[chunk, part]
-                ).start()
-            else:
-                pltpu.make_async_remote_copy(
-                    src_ref=block(work, there, chunk),
-                    dst_ref=circles.at[chunk, part],
-                    send_sem=send_sem.at[chunk, there],
-                    recv_sem=recv_sem.at[chunk, part],
-                    device_id=(there, band),
-                    device_id_type=MESH,
-                ).start()
+
+        here, landed = circles.at[chunk, part], recv_sem.at[chunk, part]
+        for i, there in enumerate(far):
+            send(there + parts, part, helper, relay.at[chunk, i], relay_recv.at[chunk, i])
+            send(there, there, band, here, landed)
+        for there in (sibling, part):
+            send(there + parts, there, helper, here, landed)
+        send(sibling, sibling, band, here, landed)
+        pltpu.make_async_copy(block(work, me, chunk), here, landed).start()
 
     span = 2 * per
     for begin in range(0, levels, span):
@@ -412,6 +411,20 @@
 
     @pl.loop(0, chunks)
     def _(chunk):
+        @pl.when(jnp.logical_not(polar))
+        def _():
+            for i, there in enumerate(far):
+                slot = relay.at[chunk, i]
+                pltpu.make_async_copy(slot, slot, relay_recv.at[chunk, i]).wait()
+                pltpu.make_async_remote_copy(
+                    src_ref=slot,
+                    dst_ref=circles.at[chunk, part],
+                    send_sem=relay_send.at[chunk, i],
+                    recv_sem=recv_sem.at[chunk, part],
+                    device_id=(there, band),
+                    device_id_type=MESH,
+                ).start()
+
         for i in range(parts):
             slot = circles.at[chunk, i]
             pltpu.make_async_copy(slot, slot, recv_sem.at[chunk, i]).wait()
@@ -511,6 +524,8 @@
         @pl.when(jnp.logical_not(polar))
         def _():
             drain(results.at[chunk, part], back_send_sem.at[chunk, part])
+            for i in range(2):
+                drain(relay.at[chunk, i], relay_send.at[chunk, i])
 
         @pl.when(polar)
         def _():
@@ -566,6 +581,7 @@
             pltpu.VMEM((2, pairs, width), jnp.float32),
             pltpu.VMEM((components, rows_here + 16, width), jnp.float32),
             pltpu.VMEM(state.shape, jnp.float32),
+            pltpu.VMEM((chunks, 2, per, rows, quarter), jnp.float32),
             pltpu.SemaphoreType.DMA((chunks, 2 * parts)),
             pltpu.SemaphoreType.DMA((chunks, parts)),
             pltpu.SemaphoreType.DMA((chunks, parts)),
@@ -573,6 +589,8 @@
             pltpu.SemaphoreType.DMA((2,)),
             pltpu.SemaphoreType.DMA((4,)),
             pltpu.SemaphoreType.DMA((4,)),
+            pltpu.SemaphoreType.DMA((chunks, 2)),
+            pltpu.SemaphoreType.DMA((chunks, 2)),
         ],
         compiler_params=pltpu.CompilerParams(
             collective_id=0, has_side_effects=True, vmem_limit_bytes=56 * 2**20

time: 154 us -> 154 us (level)
  no operation moved by 1% of the time
where the time goes in v2:
time: 154 us; the launch traced here: 152 us
  Pallas kernels  142 us (92%)
  local copies, waits for them, and re-layouts  8.31 us (5%)
    pallas_call x1, Pallas kernels, shared_substep(): pl.pallas_call(functools.partial(circle_kernel, bands, parts, chunks), ou...  142 us
    unnamed x3, local copies, waits for them, and re-layouts  6.98 us

profile of v2, /device:TPU:0, one launch (start us, length us, event | category | flops | bytes accessed | tf_op | source)
XLA Modules:
  0.0 152.1 jit_solution(4609772600982638970)
XLA Ops:
  0.0 0.8 dynamic-slice_convert_fusion
  0.8 1.3 copy.6.courant
  2.1 0.1 fusion.7
  2.2 0.1 multiply_dynamic-update-slice_fusion.3
  2.3 0.1 multiply_dynamic-update-slice_fusion.2
  2.4 0.1 multiply_dynamic-update-slice_fusion.1
  2.5 0.1 multiply_dynamic-update-slice_fusion.gains
  2.6 0.0 copy-start
  2.7 0.8 copy-done
  3.4 142.5 %shard_map.55 = f32[4,8,32,1440]{3,2,1,0:T(8,128)} custom-call(f32[4,8,32,1440]{3,2,1,0:T(8,128)} %state.1, f32[32,1]{1,0:T(8,128)} %copy.6.courant, f32[5,32,768]{2,1,0:T(8,128)} %copy-done, f32[4,1440]{1,0:T(4,128)} %constant.49.clone.twists, f32[1536,1536]{1,0:T(8,128)} %constant.50.clone.table), custom_call_target="tpu_custom_call" | custom-call | tf_op jit(solution)/shard_map/pallas_call | solution.py:565
  145.9 6.2 %copy.12 = f32[4,8,32,1440]{3,2,1,0:T(8,128)} copy(f32[4,8,32,1440]{3,2,1,0:T(8,128)} %shard_map.55) | data formatting | bytes 11796480
  (5 shorter events, 0.0 us)
Async XLA Ops:
  2.6 0.8 copy-start

commit v3 on v1

--- a/solution.py
+++ b/solution.py
@@ -530,7 +530,7 @@
 def shared_substep(state, courant, cutoff):
     parts, bands = lax.axis_size("lon"), lax.axis_size("lat")
     components, levels, rows_here, quarter = state.shape
-    per, rows = 2, 16
+    per, rows = 2, 32
     chunks = (components * levels // (2 * parts) // per) * (rows_here // rows)
     basis = quarter_basis(quarter)
     width = basis.shape[1]
@@ -588,7 +588,7 @@
         and components == parts
         and bands % 4 == 0
         and levels % 4 == 0
-        and rows_here % 16 == 0
+        and rows_here % 32 == 0
         and quarter % 128 == 32
     )
 

time: 154 us -> 163 us (1.058)
  Pallas kernels: 142 us -> 152 us
    pallas_call x1, Pallas kernels: 142 us -> 152 us  [shared_substep(): pl.pallas_call(functools.partial(circle_kernel, bands, parts, chunks), ou...]
where the time goes in v3:
time: 163 us; the launch traced here: 162 us
  Pallas kernels  152 us (93%)
  local copies, waits for them, and re-layouts  8.31 us (5%)
    pallas_call x1, Pallas kernels, shared_substep(): pl.pallas_call(functools.partial(circle_kernel, bands, parts, chunks), ou...  152 us
    unnamed x3, local copies, waits for them, and re-layouts  6.98 us

profile of v3, /device:TPU:0, one launch (start us, length us, event | category | flops | bytes accessed | tf_op | source)
XLA Modules:
  0.0 161.7 jit_solution(8626887918112869603)
XLA Ops:
  0.0 0.8 dynamic-slice_convert_fusion
  0.8 1.3 copy.6.courant
  2.1 0.1 fusion.7
  2.2 0.1 multiply_dynamic-update-slice_fusion.3
  2.3 0.1 multiply_dynamic-update-slice_fusion.2
  2.4 0.1 multiply_dynamic-update-slice_fusion.1
  2.5 0.1 multiply_dynamic-update-slice_fusion.gains
  2.6 0.0 copy-start
  2.7 0.8 copy-done
  3.4 152.1 %shard_map.55 = f32[4,8,32,1440]{3,2,1,0:T(8,128)} custom-call(f32[4,8,32,1440]{3,2,1,0:T(8,128)} %state.1, f32[32,1]{1,0:T(8,128)} %copy.6.courant, f32[5,32,768]{2,1,0:T(8,128)} %copy-done, f32[4,1440]{1,0:T(4,128)} %constant.49.clone.twists, f32[1536,1536]{1,0:T(8,128)} %constant.50.clone.table), custom_call_target="tpu_custom_call" | custom-call | tf_op jit(solution)/shard_map/pallas_call | solution.py:550
  155.5 6.2 %copy.12 = f32[4,8,32,1440]{3,2,1,0:T(8,128)} copy(f32[4,8,32,1440]{3,2,1,0:T(8,128)} %shard_map.55) | data formatting | bytes 11796480
  (5 shorter events, 0.0 us)
Async XLA Ops:
  2.6 0.8 copy-start
